TPU v7x, 512 devices: a whole 4x8x8 slice. The times are simulated.
512 devices in a mesh: loop: 16 (over x, z_lo), bulk: 32 (over z_hi, y, core).
Axes of the slice: x: 4, y: 8, z: 8 (z_hi: 2, z_lo: 4; z = z_hi * 4 + z_lo), core: 2. Of those that a mesh axis runs over, the one named last changes fastest.
Arguments:
- series: float32 [16896, 3072], P('loop', 'bulk'), may hold values from -64 to 64
Outputs:
- correlation: float32 [16, 1056, 16896], P(None, 'bulk', 'loop')
All inputs are finite; a program needn't handle non-finite values.
Results may differ from a plain program's by a relative error of at most 0.0011.
Values may be sent and summed in bfloat16 or wider, within the bound.
No kernel may reach another device: no remote copies, remote signals or barrier semaphores. Data moves between devices by JAX's collectives and lax.ppermute only.
A program may use at most 64 MiB of HBM per device.

v0:
```python
import jax
import jax.numpy as jnp
from jax import lax
from jax.sharding import PartitionSpec as P

TIME = 3072
epsilon = 1e-06


def standardize(rows):
    average = jnp.sum(rows, axis=1, keepdims=True) / TIME
    centered = rows - average
    variance = jnp.sum(centered * centered, axis=1, keepdims=True) / TIME
    return (centered * lax.rsqrt(variance + epsilon)).astype(jnp.bfloat16)


def on_device(series):
    n_bulk = lax.axis_size("bulk")
    rows, steps = series.shape
    share = rows // n_bulk
    pieces = lax.all_to_all(series.reshape(n_bulk, share, steps), "bulk", 0, 0, tiled=True)
    own = standardize(pieces.transpose(1, 0, 2).reshape(share, n_bulk * steps))
    block = lax.all_gather(own, "bulk", axis=0, tiled=True)
    others = lax.all_gather(own, "loop", axis=0, tiled=True)
    product = lax.dot_general(
        others, block, (((1,), (1,)), ((), ())), preferred_element_type=jnp.float32
    )
    return (product / TIME).reshape(lax.axis_size("loop"), share, rows)


def solution(mesh):
    placed = (P("loop", "bulk"),)
    return jax.shard_map(
        on_device, mesh=mesh, in_specs=placed, out_specs=P(None, "bulk", "loop"), check_vma=False
    )
```

profile of v0, /device:TPU:1, one launch (start us, length us, event | category | flops | bytes accessed | tf_op | source)
XLA Modules:
  0.0 305.6 jit_solution(10203501590802974913)
XLA Ops:
  6.5 0.0 all-gather.5.cloned.1.call-start
  6.5 1.2 copy.6
  7.8 39.9 %all_to_all.5 = f32[32,33,96]{2,1,0:T(8,128)S(1)} all-to-all(f32[32,33,96]{2,1,0:T(8,128)S(1)} %reshape.26), channel_id=1, replica_groups=mesh['loop'=16,'bulk'=32] {'bulk'}, dimensions={0} | all-to-all | bytes 811008 | tf_op jit(solution)/shard_map/all_to_all | solution.py:21
  47.7 0.2 reduce_sum.18
  47.9 0.3 multiply_reduce_fusion
  48.2 0.1 copy.7
  48.3 0.3 reshape.27
  48.6 0.8 fusion
  49.4 0.0 all-gather.5.cloned.1.call-update
  49.4 0.0 all-gather.7.cloned.1.call-start
  49.5 0.7 all-gather.7.cloned.1.call-update
  50.2 91.8 %all-gather.5.cloned.1.call-done = bf16[16,33,3072]{2,1,0:T(8,128)(2,1)} async-done(((bf16[1,33,3072]{2,1,0:T(8,128)(2,1)}), bf16[16,33,3072]{2,1,0:T(8,128)(2,1)}) %all-gather.5.cloned.1.call-update) | async-done | bytes 3244048 | tf_op jit(solution)/shard_map/all_gather | solution.py:24
  142.0 2.7 reshape.30
  144.7 134.6 %all-gather.7.cloned.1.call-done = bf16[32,33,3072]{2,1,0:T(8,128)(2,1)} async-done(((bf16[1,33,3072]{2,1,0:T(8,128)(2,1)}), bf16[32,33,3072]{2,1,0:T(8,128)(2,1)}) %all-gather.7.cloned.1.call-update) | async-done | bytes 6488080 | tf_op jit(solution)/shard_map/all_gather | solution.py:23
  279.3 7.1 %reshape.32 = bf16[1056,3072]{1,0:T(8,128)(2,1)} reshape(bf16[32,33,3072]{2,1,0:T(8,128)(2,1)} %all-gather.7.cloned.1.call-done) | data formatting | bytes 12976128
  286.4 8.7 %convolution_multiply_fusion = f32[528,1056]{1,0:T(8,128)} fusion(bf16[528,3072]{1,0:T(8,128)(2,1)S(1)} %reshape.30, bf16[1056,3072]{1,0:T(8,128)(2,1)} %reshape.32), kind=kOutput, calls=%fused_computation | convolution fusion | flops 3426255360 | bytes 11962368 | tf_op jit(solution)/shard_map/dot_general | solution.py:25
  295.1 1.8 reshape.28
  296.9 1.9 copy.8
  (3 shorter events, 0.1 us)
Async XLA Ops:
  6.5 135.5 %all-gather.5.cloned.1.call-start = ((), (), s32[]{:S(2)}) async-start(), calls=%async_computation.1 | async-start | bytes 4177920 | tf_op jit(solution)/shard_map/all_gather | solution.py:24
  49.4 229.9 %all-gather.7.cloned.1.call-start = ((), (), s32[]{:S(2)}) async-start(), calls=%async_computation.2 | async-start | bytes 8110080 | tf_op jit(solution)/shard_map/all_gather | solution.py:23
Sparse Core Ops, SparseCore 0:
  49.5 92.4 all-gather.4
  145.4 133.8 all-gather.6
where the time goes:
time: 306 us
  waiting for transfers between devices  227 us (74%)
  blocking collectives  39.9 us (13%)
  local copies, waits for them, and re-layouts  15.2 us (5%)
  between operations  13.4 us (4%)
  matrix products  8.65 us (3%)
    all_gather x1, waiting for transfers between devices, on_device(): block = lax.all_gather(own, 'bulk', axis=0, tiled=True)  135 us
    all_gather x1, waiting for transfers between devices, on_device(): others = lax.all_gather(own, 'loop', axis=0, tiled=True)  91.8 us
    all_to_all x1, blocking collectives, on_device(): lax.all_to_all(series.reshape(n_bulk, share, steps), 'bulk', 0, 0, tiled=...  39.9 us
    unnamed x3, local copies, waits for them, and re-layouts  11 us
    dot_general x1, matrix products, on_device(): lax.dot_general(others, block, (((1,), (1,)), ((), ())), preferred_elemen...  8.65 us
  transfers between devices with their start and end apart: 2, of which 2 were waited for; matrix products, arithmetic and copies ran while one was open for 1% of the time, Pallas kernels for 0%

commit v1 on v0

--- a/solution.py
+++ b/solution.py
@@ -21,7 +21,9 @@
     pieces = lax.all_to_all(series.reshape(n_bulk, share, steps), "bulk", 0, 0, tiled=True)
     own = standardize(pieces.transpose(1, 0, 2).reshape(share, n_bulk * steps))
     block = lax.all_gather(own, "bulk", axis=0, tiled=True)
-    others = lax.all_gather(own, "loop", axis=0, tiled=True)
+    others = jnp.concatenate(
+        lax.all_to_all(jnp.stack([own] * lax.axis_size("loop")), "loop", 0, 0), axis=0
+    )
     product = lax.dot_general(
         others, block, (((1,), (1,)), ((), ())), preferred_element_type=jnp.float32
     )

time: 306 us -> 223 us (0.73)
  waiting for transfers between devices: 227 us -> 0.04 us
  blocking collectives: 39.9 us -> 183 us
    all_to_all x0 -> x1, blocking collectives: none -> 143 us  [on_device(): lax.all_to_all(jnp.stack([own] * lax.axis_size('loop')), 'loop', 0, 0)]
    all_gather x1, waiting for transfers between devices: 135 us -> 0.02 us  [on_device(): block = lax.all_gather(own, 'bulk', axis=0, tiled=True)]
    all_gather x1 -> x0, waiting for transfers between devices: 91.8 us -> none  [on_device(): others = lax.all_gather(own, 'loop', axis=0, tiled=True)]
    unnamed x3 -> x2, local copies, waits for them, and re-layouts: 11 us -> 8.34 us
  transfers between devices with their start and end apart: 2 -> 1, of which waited for: 2 -> 0; matrix products, arithmetic and copies ran while one was open for 1% -> 1% of each run, Pallas kernels for 0% -> 0%
where the time goes in v1:
time: 223 us; the launch traced here: 222 us
  blocking collectives  183 us (82%)
  local copies, waits for them, and re-layouts  15.7 us (7%)
  between operations  13.5 us (6%)
  matrix products  8.65 us (4%)
    all_to_all x1, blocking collectives, on_device(): lax.all_to_all(jnp.stack([own] * lax.axis_size('loop')), 'loop', 0, 0)  143 us
    all_to_all x1, blocking collectives, on_device(): lax.all_to_all(series.reshape(n_bulk, share, steps), 'bulk', 0, 0, tiled=...  39.9 us
    dot_general x1, matrix products, on_device(): lax.dot_general(others, block, (((1,), (1,)), ((), ())), preferred_elemen...  8.65 us
    unnamed x2, local copies, waits for them, and re-layouts  8.34 us
  transfers between devices with their start and end apart: 1, of which 0 were waited for; matrix products, arithmetic and copies ran while one was open for 1% of the time, Pallas kernels for 0%

profile of v1, /device:TPU:1, one launch (start us, length us, event | category | flops | bytes accessed | tf_op | source)
XLA Modules:
  0.0 222.0 jit_solution(14022128890702746791)
XLA Ops:
  6.5 0.0 all-gather.3.cloned.1.call-start
  6.5 1.2 copy.6
  7.8 39.9 %all_to_all.10 = f32[32,33,96]{2,1,0:T(8,128)S(1)} all-to-all(f32[32,33,96]{2,1,0:T(8,128)S(1)} %reshape.44), channel_id=1, replica_groups=mesh['loop'=16,'bulk'=32] {'bulk'}, dimensions={0} | all-to-all | bytes 811008 | tf_op jit(solution)/shard_map/all_to_all | solution.py:21
  47.7 0.2 reduce_sum.18
  47.9 0.3 multiply_reduce_fusion
  48.2 0.1 copy.7
  48.3 0.3 reshape.45
  48.6 0.8 fusion.2
  49.4 0.0 all-gather.3.cloned.1.call-update
  49.4 0.1 multiply_convert_fusion
  49.5 0.5 stack.2
  50.0 142.9 %all_to_all.11 = bf16[16,33,3072]{2,1,0:T(8,128)(2,1)} all-to-all(bf16[16,33,3072]{2,1,0:T(8,128)(2,1)S(1)} %stack.2), channel_id=1, replica_groups=mesh['loop'=16,'bulk'=32] {'loop'}, dimensions={0} | all-to-all | bytes 6488064 | tf_op jit(solution)/shard_map/all_to_all | solution.py:25
  192.9 2.7 %reshape.46 = bf16[528,3072]{1,0:T(8,128)(2,1)S(1)} reshape(bf16[16,33,3072]{2,1,0:T(8,128)(2,1)} %all_to_all.11) | data formatting | bytes 6488064 | tf_op jit(solution)/shard_map/reshape | solution.py:24
  195.6 0.0 all-gather.3.cloned.1.call-done
  195.6 7.1 %reshape.49 = bf16[1056,3072]{1,0:T(8,128)(2,1)} reshape(bf16[32,33,3072]{2,1,0:T(8,128)(2,1)} %all-gather.3.cloned.1.call-done) | data formatting | bytes 12976128
  202.8 8.7 %convolution_multiply_fusion = f32[528,1056]{1,0:T(8,128)} fusion(bf16[528,3072]{1,0:T(8,128)(2,1)S(1)} %reshape.46, bf16[1056,3072]{1,0:T(8,128)(2,1)} %reshape.49), kind=kOutput, calls=%fused_computation | convolution fusion | flops 3426255360 | bytes 11962368 | tf_op jit(solution)/shard_map/dot_general | solution.py:27
  211.4 1.8 reshape.47
  213.2 1.9 copy.8
  (3 shorter events, 0.1 us)
Async XLA Ops:
  6.5 189.1 %all-gather.3.cloned.1.call-start = ((), (), s32[]{:S(2)}) async-start(), calls=%async_computation.2 | async-start | bytes 8110080 | tf_op jit(solution)/shard_map/all_gather | solution.py:23
Sparse Core Ops, SparseCore 0:
  49.5 143.5 all-gather.2
